TPU v7x, 32 devices: a whole 2x2x4 slice. The times are simulated.
32 devices in a mesh: lists: 16 (over z, x, core), sub: 2 (over y).
Axes of the slice: x: 2, y: 2, z: 4, core: 2. Of those that a mesh axis runs over, the one named last changes fastest.
Arguments:
- vectors: bfloat16 [768, 6144], P('sub', 'lists'), may hold values from -6 to 6
- list_ids: int32 [6144], P('lists'), may hold values from 0 to 63
- counts: int32 [16, 16], replicated, may hold values from 0 to 24, as said below
- coarse: bfloat16 [768, 1024], P(None, ('lists', 'sub')), may hold values from -3 to 3
- codebook_init: float32 [768, 256], P('sub'), may hold values from -6 to 6
- codes: int32 [2, 96, 6144], P(None, 'sub', 'lists'), may hold values from 0 to 255
Outputs:
- codebook: float32 [768, 256], P('sub')
- leftover: bfloat16 [768, 6144], P('sub', 'lists')
Inputs may be any that keep to these rules, and one draw needn't show every extreme that they name: `counts`: counts of used slots in each block; in every draw one owner receives full blocks of 24 from every sender. `list_ids`: every slot names one of its block owner's lists.
All inputs are finite; a program needn't handle non-finite values.
Results may differ from a plain program's by a relative error of at most 0.0051.
Values may be sent and summed in bfloat16 or wider, within the bound.
A program may use at most 64 MiB of HBM per device.

v0:
```python
import jax
import jax.numpy as jnp
from jax import lax
from jax.sharding import PartitionSpec as P

K = 256
DS = 8
LISTS_DEV = 64
ITERS = 2


def shards(vectors, list_ids, counts, coarse, codebook_init, codes):
    features, rows = vectors.shape
    owners = lax.axis_size("lists")
    owner = lax.axis_index("lists")
    block = rows // owners
    subspaces = features // DS
    mine = lax.all_to_all(coarse, "sub", split_axis=0, concat_axis=1, tiled=True)
    list_iota = jnp.arange(LISTS_DEV, dtype=jnp.int32)
    arrived = lax.all_to_all(vectors, "lists", split_axis=1, concat_axis=1, tiled=True)
    labels = lax.all_to_all(
        list_ids.reshape(1, rows), "lists", split_axis=1, concat_axis=1, tiled=True
    ).reshape(rows)
    selector = (labels[None, :] == list_iota[:, None]).astype(jnp.bfloat16)
    centre = jnp.dot(mine, selector, preferred_element_type=jnp.float32)
    residual = (arrived.astype(jnp.float32) - centre).astype(jnp.bfloat16)
    block_counts = lax.dynamic_index_in_dim(counts, owner, 1, keepdims=False)
    valid = (jnp.arange(block, dtype=jnp.int32)[None, :] < block_counts[:, None]).reshape(rows)
    code_iota = jnp.arange(K, dtype=jnp.int32)
    split_res = residual.reshape(subspaces, DS, rows)
    group_size = 4
    groups = subspaces // group_size
    grouped_res = split_res.reshape(groups, group_size, DS, rows)
    grouped_codes = jnp.swapaxes(codes, 0, 1).reshape(groups, group_size, ITERS, rows)

    def group_sums(packed):
        sub_res, sub_codes = packed
        one_hot = (sub_codes[:, :, None, :] == code_iota[None, None, :, None]) & valid[
            None, None, None, :
        ]
        one_hot = one_hot.astype(jnp.bfloat16)
        sums = jnp.einsum("gdr,gtkr->tgdk", sub_res, one_hot, preferred_element_type=jnp.float32)
        tally = jnp.swapaxes(jnp.sum(one_hot, axis=3, dtype=jnp.float32), 0, 1)
        return (sums, tally)

    part_sums, part_counts = lax.map(group_sums, (grouped_res, grouped_codes))
    part_sums = jnp.swapaxes(part_sums, 0, 1).reshape(ITERS, features, K)
    part_counts = jnp.swapaxes(part_counts, 0, 1).reshape(ITERS, subspaces, K)
    weight = 0.25 * jnp.sum(counts).astype(jnp.float32) / K
    total_sums, total_counts = lax.psum((part_sums, part_counts), "lists")
    codebook = codebook_init
    for iteration in range(ITERS):
        spread = jnp.repeat(total_counts[iteration], DS, axis=0)
        codebook = (total_sums[iteration] + weight * codebook) / (spread + weight)
    final_codes = codes[ITERS - 1]
    split_book = codebook.reshape(subspaces, DS, K)
    index_table = jnp.broadcast_to(final_codes[:, None, :], (subspaces, DS, rows))
    picked = jnp.take_along_axis(split_book, index_table, axis=2)
    leftover = jnp.where(valid[None, None, :], split_res.astype(jnp.float32) - picked, 0.0)
    leftover = leftover.astype(jnp.bfloat16).reshape(features, rows)
    return (codebook, leftover)


def solution(mesh):
    return jax.shard_map(
        shards,
        mesh=mesh,
        in_specs=(
            P("sub", "lists"),
            P("lists"),
            P(),
            P(None, ("lists", "sub")),
            P("sub", None),
            P(None, "sub", "lists"),
        ),
        out_specs=(P("sub", None), P("sub", "lists")),
        check_vma=False,
    )
```

profile of v0, /device:TPU:0, one launch (start us, length us, event | category | flops | bytes accessed | tf_op | source)
XLA Modules:
  0.0 1309.6 jit_solution(1981904444986645800)
XLA Ops:
  7.2 1.4 all_to_all.28
  8.6 7.4 all-to-all-start.1
  16.0 1.9 copy.22
  17.8 4.5 all-to-all-done.1
  22.3 3.5 all-to-all-start
  25.9 0.6 copy.33
  29.2 7.2 all-to-all-done
  36.4 3.3 all-to-all-start.2
  40.0 3.7 all-to-all-done.2
  44.0 25.3 %while.13 = (s32[]{:T(128)}, f32[12,2,4,8,256]{4,3,1,2,0:T(8,128)S(1)}, f32[12,2,4,256]{3,1,2,0:T(2,128)}, s32[12,4,2,384]{3,2,1,0:T(2,128)S(1)}, bf16[12,4,8,38...) while((s32[]{:T(128)}, f32[12,2,4,8,256]{4,3,1,2,0:T(8,128)S(1)}, ...), condition=%wide.region_2.3_spmd.clone, body=%wide.region_0.2_spmd.clone.sunk | while | flops 18086272 | bytes 167569 | solution.py:46
  44.2 0.7 fusion.36
  44.9 0.6 convert_reduce_fusion.2
  45.5 0.6 bitcast_dynamic-update-slice_fusion.2
  46.3 0.7 fusion.36
  47.0 0.6 convert_reduce_fusion.2
  47.6 0.6 bitcast_dynamic-update-slice_fusion.2
  48.4 0.7 fusion.36
  49.1 0.6 convert_reduce_fusion.2
  50.5 0.7 fusion.36
  51.2 0.6 convert_reduce_fusion.2
  51.8 0.6 bitcast_dynamic-update-slice_fusion.2
  52.6 0.7 fusion.36
  53.3 0.6 convert_reduce_fusion.2
  54.7 0.7 fusion.36
  55.4 0.6 convert_reduce_fusion.2
  56.0 0.6 bitcast_dynamic-update-slice_fusion.2
  56.8 0.7 fusion.36
  57.5 0.6 convert_reduce_fusion.2
  58.9 0.7 fusion.36
  59.6 0.6 convert_reduce_fusion.2
  61.0 0.7 fusion.36
  61.7 0.6 convert_reduce_fusion.2
  62.3 0.6 bitcast_dynamic-update-slice_fusion.2
  63.1 0.7 fusion.36
  63.8 0.6 convert_reduce_fusion.2
  65.2 0.7 fusion.36
  65.9 0.6 convert_reduce_fusion.2
  66.5 0.6 bitcast_dynamic-update-slice_fusion.2
  67.3 0.7 fusion.36
  68.0 0.6 convert_reduce_fusion.2
  69.2 1.0 copy.25
  70.7 0.6 lt.43
  71.3 89.8 %all-reduce.3.cloned.1.call-done = (f32[2,384,256]{2,1,0:T(8,128)}, f32[2,48,256]{2,0,1:T(2,128)}) async-done(((f32[2,384,256]{2,1,0:T(8,128)}, f32[2,48,256]{2,0,1:T(2,128)}), (f32[2,384,256]{2,1,0:T(8,128)}, f32[2,48,256]{2,0,1:T(2,128)})) %all-reduce.3.cloned.1.call-update) | async-done | bytes 884752 | tf_op jit(solution)/shard_map/psum | solution.py:50
  161.1 1.1 slice_add_fusion.1
  162.1 1.3 fusion.28
  163.4 1137.4 %gather_fusion = f32[147456]{0:T(1024)S(1)} fusion(f32[48,8,256]{2,1,0:T(8,128)S(1)} %bitcast.94, s32[147456]{0:T(1024)S(1)} %reshape.85), kind=kCustom, calls=%fused_computation | custom fusion | bytes 2949120 | tf_op jit(solution)/shard_map/jit(take_along_axis)/gather | solution.py:58
  1301.0 0.8 copy-done.2
  1301.8 0.9 fusion.22
  (90 shorter events, 9.0 us)
Async XLA Ops:
  7.2 18.7 %copy-start.3 = (s32[2,48,384]{2,1,0:T(8,128)S(1)}, s32[2,48,384]{2,1,0:T(8,128)}, u32[]{:S(2)}) copy-start(s32[2,48,384]{2,1,0:T(8,128)} %param.13) | copy-start | bytes 442372
  7.2 18.7 %copy-start.11 = (bf16[768,32]{0,1:T(8,128)(2,1)S(1)}, bf16[768,32]{0,1:T(8,128)(2,1)}, u32[]{:S(2)}) copy-start(bf16[768,32]{0,1:T(8,128)(2,1)} %param.11) | copy-start | bytes 147460
  8.6 13.7 %all-to-all-start.1 = ((s32[1,16,24]{2,0,1:T(1,128)}), s32[1,16,24]{2,0,1:T(1,128)S(1)}, u32[]{:S(2)}, u32[]{:S(2)}) async-start(s32[1,16,24]{2,0,1:T(1,128)} %all_to_all.28), calls=%async_computation.1 | async-start | bytes 16384 | tf_op jit(solution)/shard_map/all_to_all | solution.py:21
  16.0 10.7 copy-start.12
  22.3 14.1 %all-to-all-start = ((bf16[384,16,24]{0,2,1:T(8,128)(2,1)}), bf16[384,16,24]{0,2,1:T(8,128)(2,1)S(1)}, u32[]{:S(2)}, u32[]{:S(2)}) async-start(bf16[384,16,24]{0,2,1:T(8,128)(2,1)} %bitcast.2), calls=%async_computation | async-start | bytes 589824 | tf_op jit(solution)/shard_map/all_to_all | solution.py:20
  25.9 44.4 %copy-start.9 = (pred[48,384]{1,0:T(8,128)(4,1)}, pred[48,384]{1,0:T(8,128)(4,1)S(1)}, u32[]{:S(2)}) copy-start(pred[48,384]{1,0:T(8,128)(4,1)S(1)} %broadcast_compare_fusion) | copy-start | bytes 55300
  28.0 42.3 %copy-start.4 = (s32[48,384]{1,0:T(8,128)}, s32[48,384]{1,0:T(8,128)S(1)}, u32[]{:S(2)}) copy-start(s32[48,384]{1,0:T(8,128)S(1)} %broadcast_add_fusion) | copy-start | bytes 221188
  28.0 42.3 %copy-start.6 = (s32[48,384]{1,0:T(8,128)}, s32[48,384]{1,0:T(8,128)S(1)}, u32[]{:S(2)}) copy-start(s32[48,384]{1,0:T(8,128)S(1)} %slice_bitcast_fusion.2) | copy-start | bytes 221188
  36.4 7.3 all-to-all-start.2
  39.7 121.4 %all-reduce.3.cloned.1.call-start = ((), (), s32[]{:S(2)}) async-start(), calls=%async_computation.3 | async-start | bytes 1769472 | tf_op jit(solution)/shard_map/psum | solution.py:50
  69.2 1.0 copy-start.1
  70.5 91.6 %copy-start.8 = (f32[384,256]{1,0:T(8,128)S(1)}, f32[384,256]{1,0:T(8,128)}, u32[]{:S(2)}) copy-start(f32[384,256]{1,0:T(8,128)} %param.12) | copy-start | bytes 1179652
  163.4 1137.4 %copy-start = (f32[384,256]{1,0:T(8,128)}, f32[384,256]{1,0:T(8,128)S(1)}, u32[]{:S(2)}) copy-start(f32[384,256]{1,0:T(8,128)S(1)} %fusion.28) | copy-start | bytes 1179652
  1300.8 1.0 copy-start.2
  1300.8 1.0 copy-start.5
  1300.8 1.0 copy-start.7
  1300.8 1.0 copy-start.10
  1300.8 1.0 copy-start.13
Sparse Core Ops, SparseCore 0:
  70.4 90.6 all-reduce.2
where the time goes:
time: 1310 us
  local copies, waits for them, and re-layouts  1150 us (88%)
  waiting for transfers between devices  105 us (8%)
  between operations  14.9 us (1%)
  starting transfers between devices  14.2 us (1%)
  other arithmetic  13.2 us (1%)
    gather x3, local copies, waits for them, and re-layouts, shards(): picked = jnp.take_along_axis(split_book, index_table, axis=2)  1140 us
    psum x1, waiting for transfers between devices, shards(): total_sums, total_counts = lax.psum((part_sums, part_counts), 'lists')  89.8 us
  transfers between devices with their start and end apart: 4, of which 4 were waited for; matrix products, arithmetic and copies ran while one was open for 0% of the time, Pallas kernels for 0%

commit v1 on v0

--- a/solution.py
+++ b/solution.py
@@ -52,10 +52,20 @@
     for iteration in range(ITERS):
         spread = jnp.repeat(total_counts[iteration], DS, axis=0)
         codebook = (total_sums[iteration] + weight * codebook) / (spread + weight)
-    final_codes = codes[ITERS - 1]
-    split_book = codebook.reshape(subspaces, DS, K)
-    index_table = jnp.broadcast_to(final_codes[:, None, :], (subspaces, DS, rows))
-    picked = jnp.take_along_axis(split_book, index_table, axis=2)
+    high = codebook.astype(jnp.bfloat16)
+    low = (codebook - high.astype(jnp.float32)).astype(jnp.bfloat16)
+    books = jnp.concatenate(
+        [high.reshape(subspaces, DS, K), low.reshape(subspaces, DS, K)], axis=1
+    ).reshape(groups, group_size, 2 * DS, K)
+
+    def group_pick(packed):
+        book, sub_codes = packed
+        one_hot = (sub_codes[:, None, :] == code_iota[None, :, None]).astype(jnp.bfloat16)
+        both = jnp.einsum("gdk,gkr->gdr", book, one_hot, preferred_element_type=jnp.float32)
+        return both[:, :DS] + both[:, DS:]
+
+    picked = lax.map(group_pick, (books, grouped_codes[:, :, ITERS - 1]))
+    picked = picked.reshape(subspaces, DS, rows)
     leftover = jnp.where(valid[None, None, :], split_res.astype(jnp.float32) - picked, 0.0)
     leftover = leftover.astype(jnp.bfloat16).reshape(features, rows)
     return (codebook, leftover)

time: 1310 us -> 177 us (0.14)
  local copies, waits for them, and re-layouts: 1150 us -> 14.8 us
    gather x3 -> x0, local copies, waits for them, and re-layouts: 1140 us -> none  [shards(): picked = jnp.take_along_axis(split_book, index_table, axis=2)]
  transfers between devices with their start and end apart: 4 -> 4, of which waited for: 4 -> 4; matrix products, arithmetic and copies ran while one was open for 0% -> 3% of each run, Pallas kernels for 0% -> 0%
where the time goes in v1:
time: 177 us
  waiting for transfers between devices  106 us (60%)
  local copies, waits for them, and re-layouts  14.8 us (8%)
  between operations  14.8 us (8%)
  starting transfers between devices  14.2 us (8%)
  other arithmetic  13.8 us (8%)
  matrix products  12.8 us (7%)
    psum x1, waiting for transfers between devices, shards(): total_sums, total_counts = lax.psum((part_sums, part_counts), 'lists')  90.5 us
    dot_general x12, matrix products, group_sums(): jnp.einsum('gdr,gtkr->tgdk', sub_res, one_hot, preferred_element_type=jnp...  8.24 us
    reduce_sum x12, other arithmetic, group_sums(): tally = jnp.swapaxes(jnp.sum(one_hot, axis=3, dtype=jnp.float32), 0, 1)  7.52 us
    all_to_all x1, starting transfers between devices, shards(): lax.all_to_all(list_ids.reshape(1, rows), 'lists', split_axis=1, concat_a...  7.36 us
    dynamic_update_slice x12, local copies, waits for them, and re-layouts, shards(): part_sums, part_counts = lax.map(group_sums, (grouped_res, grouped_codes))  7.27 us
    all_to_all x1, waiting for transfers between devices, shards(): lax.all_to_all(vectors, 'lists', split_axis=1, concat_axis=1, tiled=True)  7 us
    all_to_all x1, waiting for transfers between devices, shards(): lax.all_to_all(list_ids.reshape(1, rows), 'lists', split_axis=1, concat_a...  4.47 us
    dot_general x12, matrix products, group_pick(): jnp.einsum('gdk,gkr->gdr', book, one_hot, preferred_element_type=jnp.floa...  4.29 us
  transfers between devices with their start and end apart: 4, of which 4 were waited for; matrix products, arithmetic and copies ran while one was open for 3% of the time, Pallas kernels for 0%

profile of v1, /device:TPU:0, one launch (start us, length us, event | category | flops | bytes accessed | tf_op | source)
XLA Modules:
  0.0 176.7 jit_solution(4619838477152994786)
XLA Ops:
  7.2 1.4 all_to_all.28
  8.6 7.4 %all-to-all-start.1 = ((s32[1,16,24]{2,0,1:T(1,128)}), s32[1,16,24]{2,0,1:T(1,128)S(1)}, u32[]{:S(2)}, u32[]{:S(2)}) async-start(s32[1,16,24]{2,0,1:T(1,128)} %all_to_all.28), calls=%async_computation.1 | async-start | bytes 16384 | tf_op jit(solution)/shard_map/all_to_all | solution.py:21
  16.0 1.9 %copy.21 = bf16[384,384]{0,1:T(8,128)(2,1)} copy(bf16[384,384]{1,0:T(8,128)(2,1)} %param.10) | data formatting | bytes 589824 | tf_op args[0]
  17.8 4.5 %all-to-all-done.1 = s32[1,16,24]{2,0,1:T(1,128)S(1)} async-done(((s32[1,16,24]{2,0,1:T(1,128)}), s32[1,16,24]{2,0,1:T(1,128)S(1)}, u32[]{:S(2)}, u32[]{:S(2)}) %all-to-all-start.1) | async-done | bytes 1568 | tf_op jit(solution)/shard_map/all_to_all | solution.py:21
  22.3 3.5 %all-to-all-start = ((bf16[384,16,24]{0,2,1:T(8,128)(2,1)}), bf16[384,16,24]{0,2,1:T(8,128)(2,1)S(1)}, u32[]{:S(2)}, u32[]{:S(2)}) async-start(bf16[384,16,24]{0,2,1:T(8,128)(2,1)} %bitcast.1), calls=%async_computation | async-start | bytes 589824 | tf_op jit(solution)/shard_map/all_to_all | solution.py:20
  25.9 0.6 copy.36
  26.6 0.7 reduce_sum.18
  28.6 0.6 reduce.5
  29.4 7.0 %all-to-all-done = bf16[384,16,24]{0,2,1:T(8,128)(2,1)S(1)} async-done(((bf16[384,16,24]{0,2,1:T(8,128)(2,1)}), bf16[384,16,24]{0,2,1:T(8,128)(2,1)S(1)}, u32[]{:S(2)}, u32[]{:S(2)}) %all-to-all-start) | async-done | bytes 294944 | tf_op jit(solution)/shard_map/all_to_all | solution.py:20
  36.4 3.3 %all-to-all-start.2 = ((bf16[2,384,32]{1,2,0:T(8,128)(2,1)}), bf16[2,384,32]{1,2,0:T(8,128)(2,1)S(1)}, u32[]{:S(2)}, u32[]{:S(2)}) async-start(bf16[2,384,32]{1,2,0:T(8,128)(2,1)} %bitcast.93), calls=%async_computation.2 | async-start | bytes 98304 | tf_op jit(solution)/shard_map/all_to_all | solution.py:18
  40.0 3.7 %all-to-all-done.2 = bf16[2,384,32]{1,2,0:T(8,128)(2,1)S(1)} async-done(((bf16[2,384,32]{1,2,0:T(8,128)(2,1)}), bf16[2,384,32]{1,2,0:T(8,128)(2,1)S(1)}, u32[]{:S(2)}, u32[]{:S(2)}) %all-to-all-start.2) | async-done | bytes 49184 | tf_op jit(solution)/shard_map/all_to_all | solution.py:18
  44.0 25.4 %while.24 = (s32[]{:T(128)}, f32[12,2,4,8,256]{4,3,1,2,0:T(8,128)S(1)}, f32[12,2,4,256]{3,1,2,0:T(2,128)}, s32[12,4,2,384]{3,1,0,2:T(4,128)S(1)}, bf16[12,4,8,38...) while((s32[]{:T(128)}, f32[12,2,4,8,256]{4,3,1,2,0:T(8,128)S(1)}, ...), condition=%wide.region_2.3_spmd.clone, body=%wide.region_0.2_spmd.clone.sunk | while | flops 18086272 | bytes 192145 | solution.py:46
  44.2 0.7 fusion.48
  44.9 0.6 convert_reduce_fusion.2
  45.5 0.6 bitcast_dynamic-update-slice_fusion.2
  46.3 0.7 fusion.48
  47.0 0.6 convert_reduce_fusion.2
  48.4 0.7 fusion.48
  49.1 0.6 convert_reduce_fusion.2
  49.7 0.6 bitcast_dynamic-update-slice_fusion.2
  50.5 0.7 fusion.48
  51.2 0.6 convert_reduce_fusion.2
  51.8 0.6 bitcast_dynamic-update-slice_fusion.2
  52.6 0.7 fusion.48
  53.3 0.6 convert_reduce_fusion.2
  54.8 0.7 fusion.48
  55.4 0.6 convert_reduce_fusion.2
  56.9 0.7 fusion.48
  57.6 0.6 convert_reduce_fusion.2
  58.2 0.6 bitcast_dynamic-update-slice_fusion.2
  59.0 0.7 fusion.48
  59.7 0.6 convert_reduce_fusion.2
  60.3 0.6 bitcast_dynamic-update-slice_fusion.2
  61.1 0.7 fusion.48
  61.8 0.6 convert_reduce_fusion.2
  63.2 0.7 fusion.48
  63.9 0.6 convert_reduce_fusion.2
  65.3 0.7 fusion.48
  66.0 0.6 convert_reduce_fusion.2
  66.6 0.6 bitcast_dynamic-update-slice_fusion.2
  67.4 0.7 fusion.48
  68.1 0.6 convert_reduce_fusion.2
  69.4 1.0 copy.25
  70.6 90.5 %all-reduce.3.cloned.1.call-done = (f32[2,384,256]{2,1,0:T(8,128)}, f32[2,48,256]{2,0,1:T(2,128)}) async-done(((f32[2,384,256]{2,1,0:T(8,128)}, f32[2,48,256]{2,0,1:T(2,128)}), (f32[2,384,256]{2,1,0:T(8,128)}, f32[2,48,256]{2,0,1:T(2,128)})) %all-reduce.3.cloned.1.call-update) | async-done | bytes 884752 | tf_op jit(solution)/shard_map/psum | solution.py:50
  161.1 1.1 slice_add_fusion.2
  162.2 2.0 %subtract_convert_fusion = (bf16[384,256]{1,0:T(8,128)(2,1)S(1)}, bf16[384,256]{1,0:T(8,128)(2,1)S(1)}, f32[384,256]{1,0:T(8,128)}) fusion(f32[48,256]{1,0:T(8,128)S(1)} %get-tuple-element.147, f32[48,256]{1,0:T(8,128)S(1)} %get-tuple-element.148, f32[384,256]{1,0:T(8,128)S(1)} %copy-done, f32[2,384,256]{2,1,0:T(8,128)} %get-tuple-element.140, f32[]{:T(128)S(6)} %div.9), kind=kLoop, calls=%fused_computation.43 | loop fusion | flops 983040 | bytes 2064388 | tf_op jit(solution)/shard_map/convert_element_type | solution.py:56
  164.2 4.8 %while.25 = (s32[]{:T(128)}, f32[12,4,8,384]{3,2,1,0:T(8,128)S(1)}, bf16[12,4,16,256]{3,2,1,0:T(8,128)(2,1)S(1)}, s32[12,4,384]{2,1,0:T(4,128)S(1)}, s32[]{:T(128)}) while((s32[]{:T(128)}, f32[12,4,8,384]{3,2,1,0:T(8,128)S(1)}, bf16[12,4,16,256]{3,2,1,0:T(8,128)(2,1)S(1)}, s32[12,4,384]{2,1,0:T(4,128)S(1)}, s32[]{:T(128)}) %tuple.52), condition=%wide.region_7.8_spmd.clone, body=%wide.region_6.7_spmd.clone.sunk | while | flops 12988418 | bytes 297033 | solution.py:67
  169.0 0.8 fusion.31
  (115 shorter events, 12.1 us)
Async XLA Ops:
  7.2 18.7 %copy-start.2 = (bf16[768,32]{0,1:T(8,128)(2,1)S(1)}, bf16[768,32]{0,1:T(8,128)(2,1)}, u32[]{:S(2)}) copy-start(bf16[768,32]{0,1:T(8,128)(2,1)} %param.13) | copy-start | bytes 147460
  7.2 19.3 %copy-start.1 = (s32[2,48,384]{2,1,0:T(8,128)S(1)}, s32[2,48,384]{2,1,0:T(8,128)}, u32[]{:S(2)}) copy-start(s32[2,48,384]{2,1,0:T(8,128)} %param.15) | copy-start | bytes 442372
  8.6 13.7 %all-to-all-start.1 = ((s32[1,16,24]{2,0,1:T(1,128)}), s32[1,16,24]{2,0,1:T(1,128)S(1)}, u32[]{:S(2)}, u32[]{:S(2)}) async-start(s32[1,16,24]{2,0,1:T(1,128)} %all_to_all.28), calls=%async_computation.1 | async-start | bytes 16384 | tf_op jit(solution)/shard_map/all_to_all | solution.py:21
  16.0 10.6 %copy-start.3 = (s32[16,16]{1,0:T(8,128)S(1)}, s32[16,16]{1,0:T(8,128)}, u32[]{:S(2)}) copy-start(s32[16,16]{1,0:T(8,128)} %param.12) | copy-start | bytes 3076
  22.3 14.1 %all-to-all-start = ((bf16[384,16,24]{0,2,1:T(8,128)(2,1)}), bf16[384,16,24]{0,2,1:T(8,128)(2,1)S(1)}, u32[]{:S(2)}, u32[]{:S(2)}) async-start(bf16[384,16,24]{0,2,1:T(8,128)(2,1)} %bitcast.1), calls=%async_computation | async-start | bytes 589824 | tf_op jit(solution)/shard_map/all_to_all | solution.py:20
  36.4 7.3 %all-to-all-start.2 = ((bf16[2,384,32]{1,2,0:T(8,128)(2,1)}), bf16[2,384,32]{1,2,0:T(8,128)(2,1)S(1)}, u32[]{:S(2)}, u32[]{:S(2)}) async-start(bf16[2,384,32]{1,2,0:T(8,128)(2,1)} %bitcast.93), calls=%async_computation.2 | async-start | bytes 98304 | tf_op jit(solution)/shard_map/all_to_all | solution.py:18
  39.7 121.4 %all-reduce.3.cloned.1.call-start = ((), (), s32[]{:S(2)}) async-start(), calls=%async_computation.3 | async-start | bytes 1769472 | tf_op jit(solution)/shard_map/psum | solution.py:50
  70.3 91.8 %copy-start = (f32[384,256]{1,0:T(8,128)S(1)}, f32[384,256]{1,0:T(8,128)}, u32[]{:S(2)}) copy-start(f32[384,256]{1,0:T(8,128)} %param.14) | copy-start | bytes 1179652
Sparse Core Ops, SparseCore 0:
  70.5 90.5 all-reduce.2

commit v2 on v1

--- a/solution.py
+++ b/solution.py
@@ -1,6 +1,10 @@
+import functools
+
 import jax
 import jax.numpy as jnp
 from jax import lax
+from jax.experimental import pallas as pl
+from jax.experimental.pallas import tpu as pltpu
 from jax.sharding import PartitionSpec as P
 
 K = 256
@@ -71,9 +75,286 @@
     return (codebook, leftover)
 
 
+def remote(src, dst, send_sem, recv_sem, device):
+    return pltpu.make_async_remote_copy(
+        src_ref=src,
+        dst_ref=dst,
+        send_sem=send_sem,
+        recv_sem=recv_sem,
+        device_id=device,
+        device_id_type=pl.DeviceIdType.MESH,
+    )
+
+
+def kernel(
+    owners, subs, vec, coarse, mask, weight, init, codes,
+    book_out, left_out,
+    arrived, centres, res, parts_out, parts_in, total, books,
+    vec_send, vec_recv, cen_send, cen_recv, part_send, part_recv, book_send, book_recv,
+):
+    me = lax.axis_index("lists")
+    my_sub = lax.axis_index("sub")
+    features, rows = res.shape
+    cap = vec.shape[1] // 2
+    pieces = features // DS // owners
+    height = pieces * DS
+
+    def after(d):
+        return lax.rem(me + d, owners)
+
+    def before(d):
+        return lax.rem(me + owners - d, owners)
+
+    def sub_after(d):
+        return lax.rem(my_sub + d, subs)
+
+    barrier = pltpu.get_barrier_semaphore()
+
+    @pl.loop(1, owners)
+    def _(d):
+        pl.semaphore_signal(
+            barrier, inc=1, device_id={"lists": after(d)}, device_id_type=pl.DeviceIdType.MESH
+        )
+
+    for d in range(1, subs):
+        pl.semaphore_signal(
+            barrier, inc=1, device_id={"sub": sub_after(d)}, device_id_type=pl.DeviceIdType.MESH
+        )
+    pl.semaphore_wait(barrier, owners - 1 + subs - 1)
+
+    def cen_copy(q, slot):
+        return remote(
+            coarse.at[q], centres.at[slot], cen_send.at[q], cen_recv.at[slot], {"sub": q}
+        )
+
+    def vec_copy(p, slot):
+        return remote(
+            vec.at[p], arrived.at[slot], vec_send.at[p], vec_recv.at[slot], {"lists": p}
+        )
+
+    def part_copy(p, slot):
+        return remote(
+            parts_out.at[p], parts_in.at[slot], part_send.at[p], part_recv.at[slot], {"lists": p}
+        )
+
+    def book_copy(p, slot):
+        return remote(
+            books.at[me], books.at[slot], book_send.at[p], book_recv.at[slot], {"lists": p}
+        )
+
+    for d in range(1, subs):
+        cen_copy(sub_after(d), my_sub).start()
+
+    @pl.loop(1, owners)
+    def _(d):
+        vec_copy(after(d), me).start()
+
+    arrived[me] = vec[me]
+    centres[my_sub] = coarse[my_sub]
+    for d in range(1, subs):
+        q = sub_after(d)
+        cen_copy(q, q).wait_recv()
+
+    @pl.loop(1, owners)
+    def _(d):
+        p = before(d)
+        vec_copy(p, p).wait_recv()
+
+    half = vec.shape[2]
+    slab = arrived[...].astype(jnp.float32)
+    full = jnp.concatenate(
+        [slab[:, :cap].reshape(rows, half), slab[:, cap:].reshape(rows, half)], axis=1
+    )
+    labels = full[:, features:]
+    lanes = lax.broadcasted_iota(jnp.int32, labels.shape, 1).astype(jnp.float32)
+    selector = (labels == lanes).astype(jnp.float32).astype(jnp.bfloat16)
+    lists = centres[...].reshape(subs * centres.shape[1], features)
+    lists = jnp.concatenate(
+        [lists, jnp.zeros((labels.shape[1] - lists.shape[0], features), lists.dtype)], axis=0
+    )
+    centre = jnp.dot(selector, lists, preferred_element_type=jnp.float32)
+    residual = (full[:, :features] - centre).astype(jnp.bfloat16).astype(jnp.float32)
+    used = mask[...]
+    res[...] = jnp.where(used > 0.0, residual.T, 0.0)
+
+    def one_hot(t, m):
+        code = codes[t, pl.ds(m, 1), :]
+        iota = lax.broadcasted_iota(jnp.int32, (K, rows), 0)
+        return (code == iota).astype(jnp.float32).astype(jnp.bfloat16)
+
+    def rows_of(m):
+        return pl.ds(pl.multiple_of(m * DS, DS), DS)
+
+    def part(p, t):
+        sums = []
+        tally = jnp.zeros((DS, K), jnp.float32)
+        line = lax.broadcasted_iota(jnp.int32, (DS, K), 0)
+        for j in range(pieces):
+            m = p * pieces + j
+            left = jnp.concatenate(
+                [res[rows_of(m), :], jnp.broadcast_to(used, (DS, rows))], axis=0
+            ).astype(jnp.bfloat16)
+            both = lax.dot_general(
+                left, one_hot(t, m), (((1,), (1,)), ((), ())),
+                preferred_element_type=jnp.float32,
+            )
+            sums.append(both[:DS])
+            number = both[DS:]
+            coarse_part = jnp.floor(number * (1.0 / 128.0)) * 128.0
+            tally = jnp.where(line == j, coarse_part, tally)
+            tally = jnp.where(line == pieces + j, number - coarse_part, tally)
+        return jnp.concatenate(sums + [tally], axis=0)
+
+    @pl.loop(1, owners)
+    def _(d):
+        p = after(d)
+        for t in range(ITERS):
+            parts_out[p, t] = part(p, t).astype(jnp.bfloat16)
+        part_copy(p, me).start()
+
+    for t in range(ITERS):
+        total[t] = part(me, t)
+
+    @pl.loop(1, owners)
+    def _(d):
+        p = before(d)
+        part_copy(p, p).wait_recv()
+        for t in range(ITERS):
+            total[t] += parts_in[p, t].astype(jnp.float32)
+
+    scale = weight[...]
+    mine = []
+    for j in range(pieces):
+        book = init[rows_of(me * pieces + j), :]
+        for t in range(ITERS):
+            number = (
+                total[t, height + j : height + j + 1]
+                + total[t, height + pieces + j : height + pieces + j + 1]
+            )
+            book = (total[t, j * DS : (j + 1) * DS] + scale * book) / (number + scale)
+        mine.append(book)
+    mine = jnp.concatenate(mine, axis=0)
+    books[me] = jnp.concatenate([mine[:, : K // 2], mine[:, K // 2 :]], axis=0).astype(
+        jnp.bfloat16
+    )
+
+    @pl.loop(1, owners)
+    def _(d):
+        book_copy(after(d), me).start()
+
+    def finish(p):
+        pair = books[p].astype(jnp.float32)
+        book = jnp.concatenate([pair[:height], pair[height:]], axis=1)
+        for j in range(pieces):
+            m = p * pieces + j
+            own = book[j * DS : (j + 1) * DS]
+            book_out[rows_of(m), :] = own
+            picked = jnp.dot(
+                own.astype(jnp.bfloat16), one_hot(ITERS - 1, m),
+                preferred_element_type=jnp.float32,
+            )
+            res[rows_of(m), :] = jnp.where(used > 0.0, res[rows_of(m), :] - picked, 0.0)
+
+    finish(me)
+
+    @pl.loop(1, owners)
+    def _(d):
+        p = before(d)
+        book_copy(p, p).wait_recv()
+        finish(p)
+
+    left_out[...] = res[...].astype(jnp.bfloat16)
+
+    for d in range(1, subs):
+        cen_copy(sub_after(d), my_sub).wait_send()
+
+    @pl.loop(1, owners)
+    def _(d):
+        p = after(d)
+        vec_copy(p, me).wait_send()
+        part_copy(p, me).wait_send()
+        book_copy(p, me).wait_send()
+
+
+def fused(vectors, list_ids, counts, coarse, codebook_init, codes):
+    features, rows = vectors.shape
+    owners = lax.axis_size("lists")
+    subs = lax.axis_size("sub")
+    owner = lax.axis_index("lists")
+    cap = rows // owners
+    height = features // owners
+    width = features + 128
+    vec = jnp.concatenate(
+        [
+            vectors.T,
+            jnp.broadcast_to(list_ids[:, None], (rows, 128)).astype(jnp.bfloat16),
+        ],
+        axis=1,
+    )
+    vec = vec.reshape(owners, cap, 2, width // 2).swapaxes(1, 2)
+    vec = vec.reshape(owners, 2 * cap, width // 2)
+    per = coarse.shape[1]
+    slabs = coarse.reshape(subs, features, per).swapaxes(1, 2)
+    block_counts = lax.dynamic_index_in_dim(counts, owner, 1, keepdims=False)
+    mask = (jnp.arange(cap, dtype=jnp.int32)[None, :] < block_counts[:, None]).reshape(1, rows)
+    mask = mask.astype(jnp.float32)
+    weight = jnp.full((1, K), 0.25 * jnp.sum(counts).astype(jnp.float32) / K)
+    vmem = pl.BlockSpec(memory_space=pltpu.VMEM)
+    dma = pltpu.SemaphoreType.DMA
+    part = (owners, ITERS, height + DS, K)
+    return pl.pallas_call(
+        functools.partial(kernel, owners, subs),
+        out_shape=(
+            jax.ShapeDtypeStruct((features, K), jnp.float32),
+            jax.ShapeDtypeStruct((features, rows), jnp.bfloat16),
+        ),
+        in_specs=[vmem] * 6,
+        out_specs=(vmem, vmem),
+        scratch_shapes=[
+            pltpu.VMEM(vec.shape, jnp.bfloat16),
+            pltpu.VMEM(slabs.shape, jnp.bfloat16),
+            pltpu.VMEM((features, rows), jnp.float32),
+            pltpu.VMEM(part, jnp.bfloat16),
+            pltpu.VMEM(part, jnp.bfloat16),
+            pltpu.VMEM(part[1:], jnp.float32),
+            pltpu.VMEM((owners, 2 * height, K // 2), jnp.bfloat16),
+            dma((owners,)), dma((owners,)), dma((subs,)), dma((subs,)),
+            dma((owners,)), dma((owners,)), dma((owners,)), dma((owners,)),
+        ],
+        compiler_params=pltpu.CompilerParams(
+            collective_id=0, has_side_effects=True, vmem_limit_bytes=40 * 1024 * 1024
+        ),
+    )(vec, slabs, mask, weight, codebook_init, codes)
+
+
+def fits(owners, subs, vectors, coarse):
+    features = vectors.shape[0] // subs
+    rows = vectors.shape[1] // owners
+    spaces = features // DS
+    per = coarse.shape[1] // (owners * subs)
+    return (
+        features % 256 == 128
+        and spaces % owners == 0
+        and 2 * (spaces // owners) <= DS
+        and (features // owners + DS) % 16 == 0
+        and (rows // owners) % DS == 0
+        and per % 16 == 0
+        and per * subs <= 128
+    )
+
+
+def dispatch(owners, subs, *args):
+    whole_features = args[0].shape[0] * subs
+    sizes = (
+        jax.ShapeDtypeStruct((whole_features, args[0].shape[1] * owners), jnp.bfloat16),
+        jax.ShapeDtypeStruct((whole_features, args[3].shape[1] * owners * subs), jnp.bfloat16),
+    )
+    return (fused if fits(owners, subs, *sizes) else shards)(*args)
+
+
 def solution(mesh):
     return jax.shard_map(
-        shards,
+        functools.partial(dispatch, mesh.shape["lists"], mesh.shape["sub"]),
         mesh=mesh,
         in_specs=(
             P("sub", "lists"),

time: 177 us -> 46.6 us (0.26)
  waiting for transfers between devices: 106 us -> 0 us
  Pallas kernels: 0 us -> 38.4 us
  starting transfers between devices: 14.2 us -> 0 us
  between operations: 14.8 us -> 1.39 us
  matrix products: 12.8 us -> 0 us
  other arithmetic: 13.8 us -> 2.4 us
  local copies, waits for them, and re-layouts: 14.8 us -> 3.74 us
    psum x1 -> x0, waiting for transfers between devices: 90.5 us -> none  [shards(): total_sums, total_counts = lax.psum((part_sums, part_counts), 'lists')]
    pallas_call x0 -> x1, Pallas kernels: none -> 38.4 us  [fused(): pl.pallas_call(functools.partial(kernel, owners, subs), out_shape=(jax.Sh...]
    all_to_all x3 -> x0, waiting for transfers between devices: 15.1 us -> none  [the longest x1 7 us: shards(): lax.all_to_all(vectors, 'lists', split_axis=1, concat_axis=1, tiled=True)]
    all_to_all x3 -> x0, starting transfers between devices: 14.2 us -> none  [the longest x1 7.36 us: shards(): lax.all_to_all(list_ids.reshape(1, rows), 'lists', split_axis=1, concat_a...]
    dot_general x25 -> x0, matrix products: 12.8 us -> none  [the longest x12 8.24 us: group_sums(): jnp.einsum('gdr,gtkr->tgdk', sub_res, one_hot, preferred_element_type=jnp...]
    reduce_sum x13 -> x1, other arithmetic: 8.21 us -> 0.63 us  [fused(): weight = jnp.full((1, K), 0.25 * jnp.sum(counts).astype(jnp.float32) / K)]
    dynamic_update_slice x12 -> x0, local copies, waits for them, and re-layouts: 7.27 us -> none  [shards(): part_sums, part_counts = lax.map(group_sums, (grouped_res, grouped_codes))]
    all_to_all x3 -> x0, local copies, waits for them, and re-layouts: 2.6 us -> none  [the longest x2 1.98 us: shards(): lax.all_to_all(list_ids.reshape(1, rows), 'lists', split_axis=1, concat_a...]
  transfers between devices with their start and end apart: 4 -> 0, of which waited for: 4 -> 0; matrix products, arithmetic and copies ran while one was open for 3% -> 0% of each run, Pallas kernels for 0% -> 0%
where the time goes in v2:
time: 46.6 us; the launch traced here: 45.9 us
  Pallas kernels  38.4 us (82%)
  local copies, waits for them, and re-layouts  3.74 us (8%)
  other arithmetic  2.4 us (5%)
  between operations  1.39 us (3%)
    pallas_call x1, Pallas kernels, fused(): pl.pallas_call(functools.partial(kernel, owners, subs), out_shape=(jax.Sh...  38.4 us
    unnamed x10, local copies, waits for them, and re-layouts  3.1 us
    concatenate x1, other arithmetic, fused(): jnp.concatenate([vectors.T, jnp.broadcast_to(list_ids[:, None], (rows, 12...  1 us

profile of v2, /device:TPU:0, one launch (start us, length us, event | category | flops | bytes accessed | tf_op | source)
XLA Modules:
  0.0 45.9 jit_solution(9070360543308874486)
XLA Ops:
  0.6 0.0 copy-start.3
  0.6 0.0 copy-start.2
  0.7 0.7 %copy-done.3 = s32[16,16]{1,0:T(8,128)S(1)} copy-done((s32[16,16]{1,0:T(8,128)S(1)}, s32[16,16]{1,0:T(8,128)}, u32[]{:S(2)}) %copy-start.3) | copy-done | bytes 1048
  1.3 0.6 %reduce_sum.9 = s32[]{:T(128)} reduce(s32[16,16]{1,0:T(8,128)S(1)} %copy-done.3, s32[]{:T(128)} %constant.6.clone.1), dimensions={0,1}, to_apply=%region_0.1 | reduce | flops 255 | bytes 1032 | tf_op jit(solution)/shard_map/reduce_sum | solution.py:301
  2.6 0.2 dynamic-slice_reduce_fusion
  2.8 0.7 %convert_element_type.12 = bf16[384]{0:T(512)(128)(2,1)S(1)} convert(s32[384]{0:T(512)} %param.7) | non-fusion elementwise | flops 384 | bytes 2304 | tf_op jit(solution)/shard_map/convert_element_type | solution.py:290
  3.5 0.1 fusion
  3.6 0.1 reshape.45.mask
  3.7 0.0 copy-done.2
  3.7 1.0 %pad_maximum_fusion = bf16[384,512]{0,1:T(8,128)(2,1)S(1)} fusion(bf16[384,128]{0,1:T(8,128)(2,1)S(1)} %broadcast_in_dim.4, bf16[384,384]{0,1:T(8,128)(2,1)} %bitcast.13), kind=kLoop, calls=%fused_computation | loop fusion | flops 786432 | bytes 786432 | tf_op jit(solution)/shard_map/concatenate | solution.py:287
  4.7 0.2 copy.9
  4.9 0.1 reshape.42
  5.0 0.0 copy-start
  5.0 0.0 copy-start.1
  5.0 0.1 copy.10
  5.1 0.9 %copy-done = f32[384,256]{1,0:T(8,128)S(1)} copy-done((f32[384,256]{1,0:T(8,128)S(1)}, f32[384,256]{1,0:T(8,128)}, u32[]{:S(2)}) %copy-start) | copy-done | bytes 393240
  6.0 0.0 copy-done.1
  6.0 38.4 %shard_map.77 = (f32[384,256]{1,0:T(8,128)S(1)}, bf16[384,384]{1,0:T(8,128)(2,1)S(1)}) custom-call(bf16[16,48,256]{2,1,0:T(8,128)(2,1)S(1)} %bitcast.10, bf16[2,32,384]{2,1,0:T(8,128)(2,1)S(1)} %bitcast.11, f32[1,384]{1,0:T(1,128)S(1)} %reshape.45.mask, f32[1,256]{1,0:T(1,128)S(1)} %broadcast_in_dim.5.weight, f32[384,256]{1,0:T(8,128)S(1)} %copy-done, ...), custom_call_target="tpu_custom_call" | custom-call | tf_op jit(solution)/shard_map/pallas_call | solution.py:305
  44.4 0.7 %copy.17 = f32[384,256]{1,0:T(8,128)} copy(f32[384,256]{1,0:T(8,128)S(1)} %get-tuple-element.4) | data formatting | bytes 786432
  45.2 0.7 %copy.18 = bf16[384,384]{1,0:T(8,128)(2,1)} copy(bf16[384,384]{1,0:T(8,128)(2,1)S(1)} %get-tuple-element.5) | data formatting | bytes 589824
  (3 shorter events, 0.0 us)
Async XLA Ops:
  0.6 0.7 %copy-start.3 = (s32[16,16]{1,0:T(8,128)S(1)}, s32[16,16]{1,0:T(8,128)}, u32[]{:S(2)}) copy-start(s32[16,16]{1,0:T(8,128)} %param.8) | copy-start | bytes 3076
  0.6 3.0 %copy-start.2 = (bf16[768,32]{0,1:T(8,128)(2,1)S(1)}, bf16[768,32]{0,1:T(8,128)(2,1)}, u32[]{:S(2)}) copy-start(bf16[768,32]{0,1:T(8,128)(2,1)} %param.9) | copy-start | bytes 147460
  5.0 1.0 %copy-start = (f32[384,256]{1,0:T(8,128)S(1)}, f32[384,256]{1,0:T(8,128)}, u32[]{:S(2)}) copy-start(f32[384,256]{1,0:T(8,128)} %init.1) | copy-start | bytes 1179652
  5.0 1.0 %copy-start.1 = (s32[2,48,384]{2,1,0:T(8,128)S(1)}, s32[2,48,384]{2,1,0:T(8,128)}, u32[]{:S(2)}) copy-start(s32[2,48,384]{2,1,0:T(8,128)} %codes.1) | copy-start | bytes 442372

commit v3 on v2

--- a/solution.py
+++ b/solution.py
@@ -87,15 +87,17 @@
 
 
 def kernel(
-    owners, subs, vec, coarse, mask, weight, init, codes,
+    owners, subs, vectors, list_ids, counts, own_coarse, init_hbm, codes,
     book_out, left_out,
-    arrived, centres, res, parts_out, parts_in, total, books,
+    vec, coarse, init, hot, arrived, centres, res, parts_out, parts_in, total, books,
     vec_send, vec_recv, cen_send, cen_recv, part_send, part_recv, book_send, book_recv,
+    init_sem,
 ):
     me = lax.axis_index("lists")
     my_sub = lax.axis_index("sub")
     features, rows = res.shape
     cap = vec.shape[1] // 2
+    spaces = features // DS
     pieces = features // DS // owners
     height = pieces * DS
 
@@ -120,6 +122,17 @@
         pl.semaphore_signal(
             barrier, inc=1, device_id={"sub": sub_after(d)}, device_id_type=pl.DeviceIdType.MESH
         )
+    init_copy = pltpu.make_async_copy(init_hbm, init, init_sem)
+    init_copy.start()
+    turned = own_coarse[...].astype(jnp.float32).T
+    for q in range(subs):
+        coarse[q] = turned[:, q * features : (q + 1) * features].astype(jnp.bfloat16)
+    half = vec.shape[2]
+    tail = jnp.broadcast_to(list_ids[...].astype(jnp.float32), (2 * half - features, rows))
+    slots = jnp.concatenate([vectors[...].astype(jnp.float32), tail], axis=0).T
+    for s in range(owners):
+        slot = slots[s * cap : (s + 1) * cap]
+        vec[s] = jnp.concatenate([slot[:, :half], slot[:, half:]], axis=0).astype(jnp.bfloat16)
     pl.semaphore_wait(barrier, owners - 1 + subs - 1)
 
     def cen_copy(q, slot):
@@ -151,6 +164,31 @@
 
     arrived[me] = vec[me]
     centres[my_sub] = coarse[my_sub]
+    iota = lax.broadcasted_iota(jnp.int32, (16, rows), 0).astype(jnp.float32)
+
+    @pl.loop(0, spaces)
+    def _(m):
+        for t in range(ITERS):
+            code = codes[t, pl.ds(m, 1), :].astype(jnp.float32)
+            code = jnp.broadcast_to(code, (16, rows)).astype(jnp.bfloat16)
+            for k in range(0, K, 16):
+                same = code == (iota + k).astype(jnp.bfloat16)
+                hot[t * spaces + m, k : k + 16, :] = jnp.where(
+                    same, jnp.ones_like(code), jnp.zeros_like(code)
+                )
+
+    tallies = counts[...]
+    line = lax.broadcasted_iota(jnp.int32, tallies.shape, 1)
+    senders = jnp.sum(
+        jnp.where(line == me, tallies, 0).astype(jnp.float32), axis=1, keepdims=True
+    )
+    first = lax.broadcasted_iota(jnp.int32, (owners, rows), 0) * cap
+    place = (lax.broadcasted_iota(jnp.int32, (owners, rows), 1) - first).astype(jnp.float32)
+    inside = jnp.where(place >= 0.0, 1.0, 0.0) * jnp.where(place < senders, 1.0, 0.0)
+    used = jnp.max(inside, axis=0, keepdims=True)
+    every = jnp.sum(tallies.astype(jnp.float32), axis=1, keepdims=True)
+    scale = 0.25 * jnp.sum(every, axis=0, keepdims=True) / K
+
     for d in range(1, subs):
         q = sub_after(d)
         cen_copy(q, q).wait_recv()
@@ -160,7 +198,6 @@
         p = before(d)
         vec_copy(p, p).wait_recv()
 
-    half = vec.shape[2]
     slab = arrived[...].astype(jnp.float32)
     full = jnp.concatenate(
         [slab[:, :cap].reshape(rows, half), slab[:, cap:].reshape(rows, half)], axis=1
@@ -174,13 +211,10 @@
     )
     centre = jnp.dot(selector, lists, preferred_element_type=jnp.float32)
     residual = (full[:, :features] - centre).astype(jnp.bfloat16).astype(jnp.float32)
-    used = mask[...]
     res[...] = jnp.where(used > 0.0, residual.T, 0.0)
 
     def one_hot(t, m):
-        code = codes[t, pl.ds(m, 1), :]
-        iota = lax.broadcasted_iota(jnp.int32, (K, rows), 0)
-        return (code == iota).astype(jnp.float32).astype(jnp.bfloat16)
+        return hot[t * spaces + m]
 
     def rows_of(m):
         return pl.ds(pl.multiple_of(m * DS, DS), DS)
@@ -222,7 +256,7 @@
         for t in range(ITERS):
             total[t] += parts_in[p, t].astype(jnp.float32)
 
-    scale = weight[...]
+    init_copy.wait()
     mine = []
     for j in range(pieces):
         book = init[rows_of(me * pieces + j), :]
@@ -280,25 +314,11 @@
     features, rows = vectors.shape
     owners = lax.axis_size("lists")
     subs = lax.axis_size("sub")
-    owner = lax.axis_index("lists")
     cap = rows // owners
     height = features // owners
-    width = features + 128
-    vec = jnp.concatenate(
-        [
-            vectors.T,
-            jnp.broadcast_to(list_ids[:, None], (rows, 128)).astype(jnp.bfloat16),
-        ],
-        axis=1,
-    )
-    vec = vec.reshape(owners, cap, 2, width // 2).swapaxes(1, 2)
-    vec = vec.reshape(owners, 2 * cap, width // 2)
-    per = coarse.shape[1]
-    slabs = coarse.reshape(subs, features, per).swapaxes(1, 2)
-    block_counts = lax.dynamic_index_in_dim(counts, owner, 1, keepdims=False)
-    mask = (jnp.arange(cap, dtype=jnp.int32)[None, :] < block_counts[:, None]).reshape(1, rows)
-    mask = mask.astype(jnp.float32)
-    weight = jnp.full((1, K), 0.25 * jnp.sum(counts).astype(jnp.float32) / K)
+    half = (features + 128) // 2
+    vec = (owners, 2 * cap, half)
+    slabs = (subs, coarse.shape[1], features)
     vmem = pl.BlockSpec(memory_space=pltpu.VMEM)
     dma = pltpu.SemaphoreType.DMA
     part = (owners, ITERS, height + DS, K)
@@ -308,11 +328,15 @@
             jax.ShapeDtypeStruct((features, K), jnp.float32),
             jax.ShapeDtypeStruct((features, rows), jnp.bfloat16),
         ),
-        in_specs=[vmem] * 6,
+        in_specs=[vmem] * 4 + [pl.BlockSpec(memory_space=pl.ANY), vmem],
         out_specs=(vmem, vmem),
         scratch_shapes=[
-            pltpu.VMEM(vec.shape, jnp.bfloat16),
-            pltpu.VMEM(slabs.shape, jnp.bfloat16),
+            pltpu.VMEM(vec, jnp.bfloat16),
+            pltpu.VMEM(slabs, jnp.bfloat16),
+            pltpu.VMEM((features, K), jnp.float32),
+            pltpu.VMEM((ITERS * features // DS, K, rows), jnp.bfloat16),
+            pltpu.VMEM(vec, jnp.bfloat16),
+            pltpu.VMEM(slabs, jnp.bfloat16),
             pltpu.VMEM((features, rows), jnp.float32),
             pltpu.VMEM(part, jnp.bfloat16),
             pltpu.VMEM(part, jnp.bfloat16),
@@ -320,11 +344,12 @@
             pltpu.VMEM((owners, 2 * height, K // 2), jnp.bfloat16),
             dma((owners,)), dma((owners,)), dma((subs,)), dma((subs,)),
             dma((owners,)), dma((owners,)), dma((owners,)), dma((owners,)),
+            dma,
         ],
         compiler_params=pltpu.CompilerParams(
-            collective_id=0, has_side_effects=True, vmem_limit_bytes=40 * 1024 * 1024
+            collective_id=0, has_side_effects=True, vmem_limit_bytes=52 * 1024 * 1024
         ),
-    )(vec, slabs, mask, weight, codebook_init, codes)
+    )(vectors, list_ids.reshape(1, rows), counts, coarse, codebook_init, codes)
 
 
 def fits(owners, subs, vectors, coarse):

time: 46.6 us -> 44.7 us (0.959)
  other arithmetic: 2.4 us -> 0 us
  local copies, waits for them, and re-layouts: 3.74 us -> 5.11 us
  between operations: 1.39 us -> 0.68 us
    unnamed x10 -> x11, local copies, waits for them, and re-layouts: 3.1 us -> 4.39 us
    concatenate x1 -> x0, other arithmetic: 1 us -> none  [fused(): jnp.concatenate([vectors.T, jnp.broadcast_to(list_ids[:, None], (rows, 12...]
    convert_element_type x2 -> x0, other arithmetic: 0.76 us -> none  [the longest x1 0.69 us: fused(): jnp.broadcast_to(list_ids[:, None], (rows, 128)).astype(jnp.bfloat16)]
    reduce_sum x1 -> x0, other arithmetic: 0.63 us -> none  [fused(): weight = jnp.full((1, K), 0.25 * jnp.sum(counts).astype(jnp.float32) / K)]
    reshape x2 -> x1, local copies, waits for them, and re-layouts: 0.1 us -> 0.72 us  [fused(): list_ids.reshape(1, rows)]
where the time goes in v3:
time: 44.7 us; the launch traced here: 44 us
  Pallas kernels  38.2 us (85%)
  local copies, waits for them, and re-layouts  5.11 us (11%)
  between operations  0.68 us (2%)
    pallas_call x1, Pallas kernels, fused(): pl.pallas_call(functools.partial(kernel, owners, subs), out_shape=(jax.Sh...  38.2 us
    unnamed x11, local copies, waits for them, and re-layouts  4.39 us

profile of v3, /device:TPU:0, one launch (start us, length us, event | category | flops | bytes accessed | tf_op | source)
XLA Modules:
  0.0 44.0 jit_solution(8917789833538882725)
XLA Ops:
  0.6 0.0 copy-start.2
  0.6 0.7 %reshape.7.list_ids = s32[1,384]{1,0:T(1,128)S(1)} reshape(s32[384]{0:T(512)} %param.7) | data formatting | bytes 3072 | tf_op jit(solution)/shard_map/reshape | solution.py:352
  1.4 0.0 copy-start.3
  1.4 1.0 %copy.8.own_coarse = bf16[768,32]{1,0:T(8,128)(2,1)S(1)} copy(bf16[768,32]{0,1:T(8,128)(2,1)} %param.9) | data formatting | bytes 98304 | tf_op args[3]
  2.3 0.0 copy-done.2
  2.3 0.0 copy-done.3
  2.4 0.0 copy-start
  2.4 1.0 %copy-done = f32[384,256]{1,0:T(8,128)S(1)} copy-done((f32[384,256]{1,0:T(8,128)S(1)}, f32[384,256]{1,0:T(8,128)}, u32[]{:S(2)}) %copy-start) | copy-done | bytes 393240
  3.4 0.0 copy-start.1
  3.4 1.0 %copy-done.1 = bf16[384,384]{1,0:T(8,128)(2,1)S(1)} copy-done((bf16[384,384]{1,0:T(8,128)(2,1)S(1)}, bf16[384,384]{1,0:T(8,128)(2,1)}, u32[]{:S(2)}) %copy-start.1) | copy-done | bytes 294936
  4.3 38.2 %shard_map.77 = (f32[384,256]{1,0:T(8,128)S(1)}, bf16[384,384]{1,0:T(8,128)(2,1)S(1)}) custom-call(bf16[384,384]{1,0:T(8,128)(2,1)S(1)} %copy-done.1, s32[1,384]{1,0:T(1,128)S(1)} %reshape.7.list_ids, s32[16,16]{1,0:T(8,128)S(1)} %copy-done.3, bf16[768,32]{1,0:T(8,128)(2,1)S(1)} %copy.8.own_coarse, f32[384,256]{1,0:T(8,128)S(1)} %copy-done, ...), custom_call_target="tpu_custom_call" | custom-call | tf_op jit(solution)/shard_map/pallas_call | solution.py:325
  42.5 0.7 %copy.11 = f32[384,256]{1,0:T(8,128)} copy(f32[384,256]{1,0:T(8,128)S(1)} %get-tuple-element.4) | data formatting | bytes 786432
  43.3 0.7 %copy.12 = bf16[384,384]{1,0:T(8,128)(2,1)} copy(bf16[384,384]{1,0:T(8,128)(2,1)S(1)} %get-tuple-element.5) | data formatting | bytes 589824
Async XLA Ops:
  0.6 1.7 %copy-start.2 = (s32[2,48,384]{2,1,0:T(8,128)S(1)}, s32[2,48,384]{2,1,0:T(8,128)}, u32[]{:S(2)}) copy-start(s32[2,48,384]{2,1,0:T(8,128)} %codes.1) | copy-start | bytes 442372
  1.4 1.0 %copy-start.3 = (s32[16,16]{1,0:T(8,128)S(1)}, s32[16,16]{1,0:T(8,128)}, u32[]{:S(2)}) copy-start(s32[16,16]{1,0:T(8,128)} %counts.1) | copy-start | bytes 3076
  2.4 1.0 %copy-start = (f32[384,256]{1,0:T(8,128)S(1)}, f32[384,256]{1,0:T(8,128)}, u32[]{:S(2)}) copy-start(f32[384,256]{1,0:T(8,128)} %init_hbm.1) | copy-start | bytes 1179652
  3.4 1.0 %copy-start.1 = (bf16[384,384]{1,0:T(8,128)(2,1)S(1)}, bf16[384,384]{1,0:T(8,128)(2,1)}, u32[]{:S(2)}) copy-start(bf16[384,384]{1,0:T(8,128)(2,1)} %vectors.1) | copy-start | bytes 884740

commit v4 on v3

--- a/solution.py
+++ b/solution.py
@@ -87,16 +87,22 @@
 
 
 def kernel(
-    owners, subs, vectors, list_ids, counts, own_coarse, init_hbm, codes,
+    owners, subs, vectors_hbm, list_ids, counts, coarse_hbm, init_hbm, codes_hbm,
     book_out, left_out,
-    vec, coarse, init, hot, arrived, centres, res, parts_out, parts_in, total, books,
+    vectors, own_coarse, codes,
+    vec, coarse, init, hot, arrived, centres, res, pair_out, pair_in, kept, parts_out, parts_in,
+    total, books,
     vec_send, vec_recv, cen_send, cen_recv, part_send, part_recv, book_send, book_recv,
-    init_sem,
+    pair_send, pair_recv, load_sem,
 ):
     me = lax.axis_index("lists")
     my_sub = lax.axis_index("sub")
     features, rows = res.shape
-    cap = vec.shape[1] // 2
+    cap = rows // owners
+    chips = owners // 2
+    core = lax.rem(me, 2)
+    chip = me // 2
+    partner = chip * 2 + 1 - core
     spaces = features // DS
     pieces = features // DS // owners
     height = pieces * DS
@@ -110,6 +116,15 @@
     def sub_after(d):
         return lax.rem(my_sub + d, subs)
 
+    loads = [
+        pltpu.make_async_copy(src, dst, load_sem.at[i])
+        for i, (src, dst) in enumerate(
+            ((vectors_hbm, vectors), (coarse_hbm, own_coarse), (codes_hbm, codes), (init_hbm, init))
+        )
+    ]
+    for load in loads:
+        load.start()
+
     barrier = pltpu.get_barrier_semaphore()
 
     @pl.loop(1, owners)
@@ -122,17 +137,21 @@
         pl.semaphore_signal(
             barrier, inc=1, device_id={"sub": sub_after(d)}, device_id_type=pl.DeviceIdType.MESH
         )
-    init_copy = pltpu.make_async_copy(init_hbm, init, init_sem)
-    init_copy.start()
+    loads[0].wait()
+    loads[1].wait()
     turned = own_coarse[...].astype(jnp.float32).T
     for q in range(subs):
         coarse[q] = turned[:, q * features : (q + 1) * features].astype(jnp.bfloat16)
-    half = vec.shape[2]
-    tail = jnp.broadcast_to(list_ids[...].astype(jnp.float32), (2 * half - features, rows))
+    tail = jnp.broadcast_to(list_ids[...].astype(jnp.float32), (128, rows))
     slots = jnp.concatenate([vectors[...].astype(jnp.float32), tail], axis=0).T
+    group = lax.broadcasted_iota(jnp.int32, (DS, 128), 1) // 32
     for s in range(owners):
         slot = slots[s * cap : (s + 1) * cap]
-        vec[s] = jnp.concatenate([slot[:, :half], slot[:, half:]], axis=0).astype(jnp.bfloat16)
+        label = jnp.zeros((DS, 128), jnp.float32)
+        for i in range(cap // DS):
+            label = jnp.where(group == i, slot[i * DS : (i + 1) * DS, features:], label)
+        pack = [slot[:, c : c + 128] for c in range(0, features, 128)] + [label]
+        vec[s] = jnp.concatenate(pack, axis=0).astype(jnp.bfloat16)
     pl.semaphore_wait(barrier, owners - 1 + subs - 1)
 
     def cen_copy(q, slot):
@@ -145,10 +164,19 @@
             vec.at[p], arrived.at[slot], vec_send.at[p], vec_recv.at[slot], {"lists": p}
         )
 
-    def part_copy(p, slot):
+    def pair_copy(c):
         return remote(
-            parts_out.at[p], parts_in.at[slot], part_send.at[p], part_recv.at[slot], {"lists": p}
-        )
+            pair_out.at[c], pair_in.at[c], pair_send.at[c], pair_recv.at[c], {"lists": partner}
+        )
+
+    def part_copy(c, slot):
+        return remote(
+            parts_out.at[c], parts_in.at[slot], part_send.at[c], part_recv.at[slot],
+            {"lists": c * 2 + core},
+        )
+
+    def chip_after(d):
+        return lax.rem(chip + d, chips)
 
     def book_copy(p, slot):
         return remote(
@@ -164,6 +192,7 @@
 
     arrived[me] = vec[me]
     centres[my_sub] = coarse[my_sub]
+    loads[2].wait()
     iota = lax.broadcasted_iota(jnp.int32, (16, rows), 0).astype(jnp.float32)
 
     @pl.loop(0, spaces)
@@ -200,9 +229,20 @@
 
     slab = arrived[...].astype(jnp.float32)
     full = jnp.concatenate(
-        [slab[:, :cap].reshape(rows, half), slab[:, cap:].reshape(rows, half)], axis=1
-    )
-    labels = full[:, features:]
+        [
+            slab[:, i * cap : (i + 1) * cap].reshape(rows, 128)
+            for i in range(features // 128)
+        ],
+        axis=1,
+    )
+    packed = slab[:, features // 128 * cap :].reshape(owners * DS, 128)
+    labels = jnp.concatenate(
+        [
+            jnp.broadcast_to(packed[:, i * 32 : i * 32 + 1], packed.shape).reshape(owners, DS, 128)
+            for i in range(cap // DS)
+        ],
+        axis=1,
+    ).reshape(rows, 128)
     lanes = lax.broadcasted_iota(jnp.int32, labels.shape, 1).astype(jnp.float32)
     selector = (labels == lanes).astype(jnp.float32).astype(jnp.bfloat16)
     lists = centres[...].reshape(subs * centres.shape[1], features)
@@ -210,7 +250,7 @@
         [lists, jnp.zeros((labels.shape[1] - lists.shape[0], features), lists.dtype)], axis=0
     )
     centre = jnp.dot(selector, lists, preferred_element_type=jnp.float32)
-    residual = (full[:, :features] - centre).astype(jnp.bfloat16).astype(jnp.float32)
+    residual = (full - centre).astype(jnp.bfloat16).astype(jnp.float32)
     res[...] = jnp.where(used > 0.0, residual.T, 0.0)
 
     def one_hot(t, m):
@@ -239,24 +279,38 @@
             tally = jnp.where(line == pieces + j, number - coarse_part, tally)
         return jnp.concatenate(sums + [tally], axis=0)
 
-    @pl.loop(1, owners)
-    def _(d):
-        p = after(d)
-        for t in range(ITERS):
-            parts_out[p, t] = part(p, t).astype(jnp.bfloat16)
-        part_copy(p, me).start()
-
+    def compute(d):
+        c = chip_after(d)
+        for t in range(ITERS):
+            pair_out[c, t] = part(c * 2 + 1 - core, t).astype(jnp.bfloat16)
+        pair_copy(c).start()
+        for t in range(ITERS):
+            kept[c, t] = part(c * 2 + core, t)
+
+    compute(1)
+
+    @pl.loop(2, chips + 1)
+    def _(d):
+        compute(d)
+        c = chip_after(d - 1)
+        pair_copy(c).wait_recv()
+        for t in range(ITERS):
+            both = kept[c, t] + pair_in[c, t].astype(jnp.float32)
+            parts_out[c, t] = both.astype(jnp.bfloat16)
+        part_copy(c, chip).start()
+
+    pair_copy(chip).wait_recv()
     for t in range(ITERS):
-        total[t] = part(me, t)
-
-    @pl.loop(1, owners)
-    def _(d):
-        p = before(d)
-        part_copy(p, p).wait_recv()
-        for t in range(ITERS):
-            total[t] += parts_in[p, t].astype(jnp.float32)
-
-    init_copy.wait()
+        total[t] = kept[chip, t] + pair_in[chip, t].astype(jnp.float32)
+
+    @pl.loop(1, chips)
+    def _(d):
+        c = lax.rem(chip + chips - d, chips)
+        part_copy(c, c).wait_recv()
+        for t in range(ITERS):
+            total[t] += parts_in[c, t].astype(jnp.float32)
+
+    loads[3].wait()
     mine = []
     for j in range(pieces):
         book = init[rows_of(me * pieces + j), :]
@@ -306,8 +360,15 @@
     def _(d):
         p = after(d)
         vec_copy(p, me).wait_send()
-        part_copy(p, me).wait_send()
         book_copy(p, me).wait_send()
+
+    @pl.loop(1, chips)
+    def _(d):
+        part_copy(chip_after(d), chip).wait_send()
+
+    @pl.loop(0, chips)
+    def _(c):
+        pair_copy(c).wait_send()
 
 
 def fused(vectors, list_ids, counts, coarse, codebook_init, codes):
@@ -316,21 +377,24 @@
     subs = lax.axis_size("sub")
     cap = rows // owners
     height = features // owners
-    half = (features + 128) // 2
-    vec = (owners, 2 * cap, half)
+    vec = (owners, features // 128 * cap + DS, 128)
     slabs = (subs, coarse.shape[1], features)
     vmem = pl.BlockSpec(memory_space=pltpu.VMEM)
+    hbm = pl.BlockSpec(memory_space=pl.ANY)
     dma = pltpu.SemaphoreType.DMA
-    part = (owners, ITERS, height + DS, K)
+    part = (owners // 2, ITERS, height + DS, K)
     return pl.pallas_call(
         functools.partial(kernel, owners, subs),
         out_shape=(
             jax.ShapeDtypeStruct((features, K), jnp.float32),
             jax.ShapeDtypeStruct((features, rows), jnp.bfloat16),
         ),
-        in_specs=[vmem] * 4 + [pl.BlockSpec(memory_space=pl.ANY), vmem],
+        in_specs=[hbm, vmem, vmem, hbm, hbm, hbm],
         out_specs=(vmem, vmem),
         scratch_shapes=[
+            pltpu.VMEM(vectors.shape, jnp.bfloat16),
+            pltpu.VMEM(coarse.shape, jnp.bfloat16),
+            pltpu.VMEM(codes.shape, jnp.int32),
             pltpu.VMEM(vec, jnp.bfloat16),
             pltpu.VMEM(slabs, jnp.bfloat16),
             pltpu.VMEM((features, K), jnp.float32),
@@ -340,14 +404,17 @@
             pltpu.VMEM((features, rows), jnp.float32),
             pltpu.VMEM(part, jnp.bfloat16),
             pltpu.VMEM(part, jnp.bfloat16),
+            pltpu.VMEM(part, jnp.float32),
+            pltpu.VMEM(part, jnp.bfloat16),
+            pltpu.VMEM(part, jnp.bfloat16),
             pltpu.VMEM(part[1:], jnp.float32),
             pltpu.VMEM((owners, 2 * height, K // 2), jnp.bfloat16),
             dma((owners,)), dma((owners,)), dma((subs,)), dma((subs,)),
-            dma((owners,)), dma((owners,)), dma((owners,)), dma((owners,)),
-            dma,
+            dma((owners // 2,)), dma((owners // 2,)), dma((owners,)), dma((owners,)),
+            dma((owners // 2,)), dma((owners // 2,)), dma((4,)),
         ],
         compiler_params=pltpu.CompilerParams(
-            collective_id=0, has_side_effects=True, vmem_limit_bytes=52 * 1024 * 1024
+            collective_id=0, has_side_effects=True, vmem_limit_bytes=60 * 1024 * 1024
         ),
     )(vectors, list_ids.reshape(1, rows), counts, coarse, codebook_init, codes)
 
@@ -358,7 +425,10 @@
     spaces = features // DS
     per = coarse.shape[1] // (owners * subs)
     return (
-        features % 256 == 128
+        features % 128 == 0
+        and owners % 2 == 0
+        and rows // owners <= 32
+        and (features // 128 * (rows // owners) + DS) % 16 == 0
         and spaces % owners == 0
         and 2 * (spaces // owners) <= DS
         and (features // owners + DS) % 16 == 0

time: 44.7 us -> 41.4 us (0.926)
  Pallas kernels: 38.2 us -> 35.1 us
    pallas_call x1, Pallas kernels: 38.2 us -> 35.1 us  [fused(): pl.pallas_call(functools.partial(kernel, owners, subs), out_shape=(jax.Sh...]
    reshape x1, local copies, waits for them, and re-layouts: 0.72 us -> 1.25 us  [fused(): list_ids.reshape(1, rows)]
    unnamed x11 -> x5, local copies, waits for them, and re-layouts: 4.39 us -> 4.14 us
where the time goes in v4:
time: 41.4 us; the launch traced here: 41.1 us
  Pallas kernels  35.1 us (85%)
  local copies, waits for them, and re-layouts  5.39 us (13%)
  between operations  0.65 us (2%)
    pallas_call x1, Pallas kernels, fused(): pl.pallas_call(functools.partial(kernel, owners, subs), out_shape=(jax.Sh...  35.1 us
    unnamed x5, local copies, waits for them, and re-layouts  4.14 us
    reshape x1, local copies, waits for them, and re-layouts, fused(): list_ids.reshape(1, rows)  1.25 us

profile of v4, /device:TPU:0, one launch (start us, length us, event | category | flops | bytes accessed | tf_op | source)
XLA Modules:
  0.0 41.1 jit_solution(18166759556177731234)
XLA Ops:
  0.6 1.2 %reshape.7.list_ids = s32[1,384]{1,0:T(1,128)} reshape(s32[384]{0:T(512)} %param.7) | data formatting | bytes 3072 | tf_op jit(solution)/shard_map/reshape | solution.py:419
  1.9 1.6 %copy.8.coarse_hbm = bf16[768,32]{1,0:T(8,128)(2,1)} copy(bf16[768,32]{0,1:T(8,128)(2,1)} %param.9) | data formatting | bytes 98304 | tf_op args[3]
  3.5 35.1 %shard_map.77 = (f32[384,256]{1,0:T(8,128)}, bf16[384,384]{1,0:T(8,128)(2,1)}) custom-call(bf16[384,384]{1,0:T(8,128)(2,1)} %vectors_hbm.1, s32[1,384]{1,0:T(1,128)} %reshape.7.list_ids, s32[16,16]{1,0:T(8,128)} %counts.1, bf16[768,32]{1,0:T(8,128)(2,1)} %copy.8.coarse_hbm, f32[384,256]{1,0:T(8,128)} %init_hbm.1, s32[2,48,384]{2,1,0:T(8,128)} %codes_hbm.1), custom_call_target="tpu_custom_call" | custom-call | tf_op jit(solution)/shard_map/pallas_call | solution.py:386
  38.5 0.0 copy-start
  38.6 1.8 %copy.11 = f32[384,256]{1,0:T(8,128)} copy(f32[384,256]{1,0:T(8,128)} %get-tuple-element.4) | data formatting | bytes 786432
  40.4 0.0 copy-done
  40.4 0.7 %copy.12 = bf16[384,384]{1,0:T(8,128)(2,1)} copy(bf16[384,384]{1,0:T(8,128)(2,1)S(1)} %copy-done) | data formatting | bytes 589824
Async XLA Ops:
  38.5 1.8 %copy-start = (bf16[384,384]{1,0:T(8,128)(2,1)S(1)}, bf16[384,384]{1,0:T(8,128)(2,1)}, u32[]{:S(2)}) copy-start(bf16[384,384]{1,0:T(8,128)(2,1)} %get-tuple-element.5) | copy-start | bytes 884740

commit v5 on v4

--- a/solution.py
+++ b/solution.py
@@ -139,10 +139,9 @@
         )
     loads[0].wait()
     loads[1].wait()
-    turned = own_coarse[...].astype(jnp.float32).T
     for q in range(subs):
-        coarse[q] = turned[:, q * features : (q + 1) * features].astype(jnp.bfloat16)
-    tail = jnp.broadcast_to(list_ids[...].astype(jnp.float32), (128, rows))
+        coarse[q] = own_coarse[:, q * features : (q + 1) * features]
+    tail = jnp.broadcast_to(list_ids[...].reshape(1, rows).astype(jnp.float32), (128, rows))
     slots = jnp.concatenate([vectors[...].astype(jnp.float32), tail], axis=0).T
     group = lax.broadcasted_iota(jnp.int32, (DS, 128), 1) // 32
     for s in range(owners):
@@ -336,7 +335,7 @@
         for j in range(pieces):
             m = p * pieces + j
             own = book[j * DS : (j + 1) * DS]
-            book_out[rows_of(m), :] = own
+            init[rows_of(m), :] = own
             picked = jnp.dot(
                 own.astype(jnp.bfloat16), one_hot(ITERS - 1, m),
                 preferred_element_type=jnp.float32,
@@ -351,6 +350,7 @@
         book_copy(p, p).wait_recv()
         finish(p)
 
+    book_out[...] = init[...].astype(jnp.bfloat16)
     left_out[...] = res[...].astype(jnp.bfloat16)
 
     for d in range(1, subs):
@@ -383,17 +383,17 @@
     hbm = pl.BlockSpec(memory_space=pl.ANY)
     dma = pltpu.SemaphoreType.DMA
     part = (owners // 2, ITERS, height + DS, K)
-    return pl.pallas_call(
+    codebook, leftover = pl.pallas_call(
         functools.partial(kernel, owners, subs),
         out_shape=(
-            jax.ShapeDtypeStruct((features, K), jnp.float32),
+            jax.ShapeDtypeStruct((features, K), jnp.bfloat16),
             jax.ShapeDtypeStruct((features, rows), jnp.bfloat16),
         ),
         in_specs=[hbm, vmem, vmem, hbm, hbm, hbm],
         out_specs=(vmem, vmem),
         scratch_shapes=[
             pltpu.VMEM(vectors.shape, jnp.bfloat16),
-            pltpu.VMEM(coarse.shape, jnp.bfloat16),
+            pltpu.VMEM(coarse.shape[::-1], jnp.bfloat16),
             pltpu.VMEM(codes.shape, jnp.int32),
             pltpu.VMEM(vec, jnp.bfloat16),
             pltpu.VMEM(slabs, jnp.bfloat16),
@@ -416,7 +416,8 @@
         compiler_params=pltpu.CompilerParams(
             collective_id=0, has_side_effects=True, vmem_limit_bytes=60 * 1024 * 1024
         ),
-    )(vectors, list_ids.reshape(1, rows), counts, coarse, codebook_init, codes)
+    )(vectors, list_ids, counts, coarse.T, codebook_init, codes)
+    return (codebook.astype(jnp.float32), leftover)
 
 
 def fits(owners, subs, vectors, coarse):

time: 41.4 us -> 38.3 us (0.925)
  local copies, waits for them, and re-layouts: 5.39 us -> 0.72 us
  other arithmetic: 0 us -> 1.74 us
    unnamed x5 -> x3, local copies, waits for them, and re-layouts: 4.14 us -> 0.72 us
    convert_element_type x0 -> x1, other arithmetic: none -> 1.74 us  [fused(): return (codebook.astype(jnp.float32), leftover)]
    reshape x1 -> x0, local copies, waits for them, and re-layouts: 1.25 us -> none  [fused(): list_ids.reshape(1, rows)]
where the time goes in v5:
time: 38.3 us; the launch traced here: 38.1 us
  Pallas kernels  35 us (91%)
  other arithmetic  1.74 us (5%)
  local copies, waits for them, and re-layouts  0.72 us (2%)
  between operations  0.65 us (2%)
    pallas_call x1, Pallas kernels, fused(): pl.pallas_call(functools.partial(kernel, owners, subs), out_shape=(jax.Sh...  35 us
    convert_element_type x1, other arithmetic, fused(): return (codebook.astype(jnp.float32), leftover)  1.74 us

profile of v5, /device:TPU:0, one launch (start us, length us, event | category | flops | bytes accessed | tf_op | source)
XLA Modules:
  0.0 38.1 jit_solution(3535825244613998539)
XLA Ops:
  0.6 35.0 %shard_map.77 = (bf16[384,256]{1,0:T(8,128)(2,1)}, bf16[384,384]{1,0:T(8,128)(2,1)}) custom-call(bf16[384,384]{1,0:T(8,128)(2,1)} %vectors_hbm.1, s32[384]{0:T(512)} %list_ids.1, s32[16,16]{1,0:T(8,128)} %counts.1, bf16[32,768]{1,0:T(8,128)(2,1)} %bitcast.1, f32[384,256]{1,0:T(8,128)} %init_hbm.1, s32[2,48,384]{2,1,0:T(8,128)} %codes_hbm.1), custom_call_target="tpu_custom_call" | custom-call | tf_op jit(solution)/shard_map/pallas_call | solution.py:386
  35.7 0.0 copy-start
  35.7 1.7 %convert_element_type.3 = f32[384,256]{1,0:T(8,128)} convert(bf16[384,256]{1,0:T(8,128)(2,1)} %get-tuple-element.4) | non-fusion elementwise | flops 98304 | bytes 589824 | tf_op jit(solution)/shard_map/convert_element_type | solution.py:420
  37.4 0.0 copy-done
  37.4 0.7 %copy.9 = bf16[384,384]{1,0:T(8,128)(2,1)} copy(bf16[384,384]{1,0:T(8,128)(2,1)S(1)} %copy-done) | data formatting | bytes 589824
Async XLA Ops:
  35.7 1.8 %copy-start = (bf16[384,384]{1,0:T(8,128)(2,1)S(1)}, bf16[384,384]{1,0:T(8,128)(2,1)}, u32[]{:S(2)}) copy-start(bf16[384,384]{1,0:T(8,128)(2,1)} %get-tuple-element.9) | copy-start | bytes 884740

commit v6 on v5

--- a/solution.py
+++ b/solution.py
@@ -107,11 +107,14 @@
     pieces = features // DS // owners
     height = pieces * DS
 
+    def spread(d, size):
+        return size // 2 + lax.div(d, 2) * (1 - 2 * lax.rem(d, 2))
+
     def after(d):
-        return lax.rem(me + d, owners)
+        return lax.rem(me + spread(d, owners), owners)
 
     def before(d):
-        return lax.rem(me + owners - d, owners)
+        return lax.rem(me + owners - spread(d, owners), owners)
 
     def sub_after(d):
         return lax.rem(my_sub + d, subs)
@@ -175,7 +178,7 @@
         )
 
     def chip_after(d):
-        return lax.rem(chip + d, chips)
+        return lax.rem(chip + spread(d, chips), chips)
 
     def book_copy(p, slot):
         return remote(
@@ -286,7 +289,7 @@
         for t in range(ITERS):
             kept[c, t] = part(c * 2 + core, t)
 
-    compute(1)
+    compute(jnp.int32(1))
 
     @pl.loop(2, chips + 1)
     def _(d):
@@ -304,7 +307,7 @@
 
     @pl.loop(1, chips)
     def _(d):
-        c = lax.rem(chip + chips - d, chips)
+        c = lax.rem(chip + chips - spread(d, chips), chips)
         part_copy(c, c).wait_recv()
         for t in range(ITERS):
             total[t] += parts_in[c, t].astype(jnp.float32)

time: 38.3 us -> 38.9 us (1.016)
  Pallas kernels: 35 us -> 35.6 us
    pallas_call x1, Pallas kernels: 35 us -> 35.6 us  [fused(): pl.pallas_call(functools.partial(kernel, owners, subs), out_shape=(jax.Sh...]
where the time goes in v6:
time: 38.9 us; the launch traced here: 38.7 us
  Pallas kernels  35.6 us (92%)
  other arithmetic  1.74 us (4%)
  local copies, waits for them, and re-layouts  0.72 us (2%)
  between operations  0.65 us (2%)
    pallas_call x1, Pallas kernels, fused(): pl.pallas_call(functools.partial(kernel, owners, subs), out_shape=(jax.Sh...  35.6 us
    convert_element_type x1, other arithmetic, fused(): return (codebook.astype(jnp.float32), leftover)  1.74 us

profile of v6, /device:TPU:0, one launch (start us, length us, event | category | flops | bytes accessed | tf_op | source)
XLA Modules:
  0.0 38.7 jit_solution(11959762446134274594)
XLA Ops:
  0.6 35.6 %shard_map.77 = (bf16[384,256]{1,0:T(8,128)(2,1)}, bf16[384,384]{1,0:T(8,128)(2,1)}) custom-call(bf16[384,384]{1,0:T(8,128)(2,1)} %vectors_hbm.1, s32[384]{0:T(512)} %list_ids.1, s32[16,16]{1,0:T(8,128)} %counts.1, bf16[32,768]{1,0:T(8,128)(2,1)} %bitcast.1, f32[384,256]{1,0:T(8,128)} %init_hbm.1, s32[2,48,384]{2,1,0:T(8,128)} %codes_hbm.1), custom_call_target="tpu_custom_call" | custom-call | tf_op jit(solution)/shard_map/pallas_call | solution.py:389
  36.2 0.0 copy-start
  36.2 1.7 %convert_element_type.3 = f32[384,256]{1,0:T(8,128)} convert(bf16[384,256]{1,0:T(8,128)(2,1)} %get-tuple-element.4) | non-fusion elementwise | flops 98304 | bytes 589824 | tf_op jit(solution)/shard_map/convert_element_type | solution.py:423
  38.0 0.0 copy-done
  38.0 0.7 %copy.9 = bf16[384,384]{1,0:T(8,128)(2,1)} copy(bf16[384,384]{1,0:T(8,128)(2,1)S(1)} %copy-done) | data formatting | bytes 589824
Async XLA Ops:
  36.2 1.8 %copy-start = (bf16[384,384]{1,0:T(8,128)(2,1)S(1)}, bf16[384,384]{1,0:T(8,128)(2,1)}, u32[]{:S(2)}) copy-start(bf16[384,384]{1,0:T(8,128)(2,1)} %get-tuple-element.9) | copy-start | bytes 884740

commit v7 on v5

--- a/solution.py
+++ b/solution.py
@@ -329,26 +329,33 @@
     def _(d):
         book_copy(after(d), me).start()
 
-    def finish(p):
-        pair = books[p].astype(jnp.float32)
-        book = jnp.concatenate([pair[:height], pair[height:]], axis=1)
-        for j in range(pieces):
-            m = p * pieces + j
-            own = book[j * DS : (j + 1) * DS]
+    def finish(senders):
+        stores = []
+        for p in senders:
+            pair = books[p].astype(jnp.float32)
+            book = jnp.concatenate([pair[:height], pair[height:]], axis=1)
+            for j in range(pieces):
+                m = p * pieces + j
+                own = book[j * DS : (j + 1) * DS]
+                picked = jnp.dot(
+                    own.astype(jnp.bfloat16), one_hot(ITERS - 1, m),
+                    preferred_element_type=jnp.float32,
+                )
+                left = jnp.where(used > 0.0, res[rows_of(m), :] - picked, 0.0)
+                stores.append((m, own, left))
+        for m, own, left in stores:
             init[rows_of(m), :] = own
-            picked = jnp.dot(
-                own.astype(jnp.bfloat16), one_hot(ITERS - 1, m),
-                preferred_element_type=jnp.float32,
-            )
-            res[rows_of(m), :] = jnp.where(used > 0.0, res[rows_of(m), :] - picked, 0.0)
-
-    finish(me)
-
-    @pl.loop(1, owners)
-    def _(d):
-        p = before(d)
-        book_copy(p, p).wait_recv()
-        finish(p)
+            res[rows_of(m), :] = left
+
+    finish([me])
+    batch = 3 if (owners - 1) % 3 == 0 else 1
+
+    @pl.loop(0, (owners - 1) // batch)
+    def _(i):
+        senders = [before(i * batch + 1 + e) for e in range(batch)]
+        for p in senders:
+            book_copy(p, p).wait_recv()
+        finish(senders)
 
     book_out[...] = init[...].astype(jnp.bfloat16)
     left_out[...] = res[...].astype(jnp.bfloat16)

time: 38.3 us -> 37.8 us (0.987)
  Pallas kernels: 35 us -> 34.4 us
    pallas_call x1, Pallas kernels: 35 us -> 34.4 us  [fused(): pl.pallas_call(functools.partial(kernel, owners, subs), out_shape=(jax.Sh...]
where the time goes in v7:
time: 37.8 us; the launch traced here: 37.6 us
  Pallas kernels  34.4 us (91%)
  other arithmetic  1.74 us (5%)
  local copies, waits for them, and re-layouts  0.72 us (2%)
  between operations  0.65 us (2%)
    pallas_call x1, Pallas kernels, fused(): pl.pallas_call(functools.partial(kernel, owners, subs), out_shape=(jax.Sh...  34.4 us
    convert_element_type x1, other arithmetic, fused(): return (codebook.astype(jnp.float32), leftover)  1.74 us

profile of v7, /device:TPU:0, one launch (start us, length us, event | category | flops | bytes accessed | tf_op | source)
XLA Modules:
  0.0 37.6 jit_solution(6976915793997650337)
XLA Ops:
  0.6 34.4 %shard_map.77 = (bf16[384,256]{1,0:T(8,128)(2,1)}, bf16[384,384]{1,0:T(8,128)(2,1)}) custom-call(bf16[384,384]{1,0:T(8,128)(2,1)} %vectors_hbm.1, s32[384]{0:T(512)} %list_ids.1, s32[16,16]{1,0:T(8,128)} %counts.1, bf16[32,768]{1,0:T(8,128)(2,1)} %bitcast.1, f32[384,256]{1,0:T(8,128)} %init_hbm.1, s32[2,48,384]{2,1,0:T(8,128)} %codes_hbm.1), custom_call_target="tpu_custom_call" | custom-call | tf_op jit(solution)/shard_map/pallas_call | solution.py:393
  35.1 0.0 copy-start
  35.1 1.7 %convert_element_type.3 = f32[384,256]{1,0:T(8,128)} convert(bf16[384,256]{1,0:T(8,128)(2,1)} %get-tuple-element.4) | non-fusion elementwise | flops 98304 | bytes 589824 | tf_op jit(solution)/shard_map/convert_element_type | solution.py:427
  36.8 0.0 copy-done
  36.8 0.7 %copy.9 = bf16[384,384]{1,0:T(8,128)(2,1)} copy(bf16[384,384]{1,0:T(8,128)(2,1)S(1)} %copy-done) | data formatting | bytes 589824
Async XLA Ops:
  35.1 1.8 %copy-start = (bf16[384,384]{1,0:T(8,128)(2,1)S(1)}, bf16[384,384]{1,0:T(8,128)(2,1)}, u32[]{:S(2)}) copy-start(bf16[384,384]{1,0:T(8,128)(2,1)} %get-tuple-element.9) | copy-start | bytes 884740
